TPU v7x, 32 devices: a whole 2x2x4 slice. The times are simulated.
32 devices in a mesh: seq: 4 (over y, x), fsdp: 8 (over z, core).
Axes of the slice: x: 2, y: 2, z: 4, core: 2. Of those that a mesh axis runs over, the one named last changes fastest.
Arguments:
- hidden_in: bfloat16 [8, 1024, 1024], P('fsdp', 'seq'), may hold values from -3 to 3
- segment_ids: int32 [8, 1024], P('fsdp', 'seq'), may hold values from 0 to 3, never falling along the last dimension, each value on 1 to 512 neighbouring positions
- ln1_gain: bfloat16 [1024], P('fsdp'), may hold values from 0.099609375 to 1.8984375
- ln1_bias: bfloat16 [1024], P('fsdp'), may hold values from -3 to 3
- w_qkv: bfloat16 [1024, 3072], P('fsdp'), may hold values from -0.1875 to 0.1875
- b_qv: bfloat16 [2, 1024], P(None, 'fsdp'), may hold values from -3 to 3
- w_out: bfloat16 [1024, 1024], P('fsdp'), may hold values from -0.5 to 0.5
- b_out: bfloat16 [1024], P('fsdp'), may hold values from -3 to 3
- ln2_gain: bfloat16 [1024], P('fsdp'), may hold values from 0.099609375 to 1.8984375
- ln2_bias: bfloat16 [1024], P('fsdp'), may hold values from -3 to 3
- w_up: bfloat16 [1024, 4096], P('fsdp'), may hold values from -0.1875 to 0.1875
- b_up: bfloat16 [4096], P('fsdp'), may hold values from -3 to 3
- w_down: bfloat16 [4096, 1024], P('fsdp'), may hold values from -0.09375 to 0.09375
- b_down: bfloat16 [1024], P('fsdp'), may hold values from -3 to 3
- cotangent: bfloat16 [8, 1024, 1024], P('fsdp', 'seq'), may hold values from -6 to 6
Outputs:
- output: bfloat16 [8, 1024, 1024], P('fsdp', 'seq')
- grad_input: bfloat16 [8, 1024, 1024], P('fsdp', 'seq')
- grad_ln1_gain: float32 [1024], P('fsdp')
- grad_ln1_bias: float32 [1024], P('fsdp')
- grad_w_qkv: float32 [1024, 3072], P('fsdp')
- grad_b_qv: float32 [2, 1024], P(None, 'fsdp')
- grad_w_out: float32 [1024, 1024], P('fsdp')
- grad_b_out: float32 [1024], P('fsdp')
- grad_ln2_gain: float32 [1024], P('fsdp')
- grad_ln2_bias: float32 [1024], P('fsdp')
- grad_w_up: float32 [1024, 4096], P('fsdp')
- grad_b_up: float32 [4096], P('fsdp')
- grad_w_down: float32 [4096, 1024], P('fsdp')
- grad_b_down: float32 [1024], P('fsdp')
Inputs may be any that keep to these rules, and one draw needn't show every extreme that they name: `segment_ids`: along each sequence the ids never fall; each of the 4 ids marks one run of consecutive tokens, the longest of them 1024 // 2 tokens.
All inputs are finite; a program needn't handle non-finite values.
Results may differ from a plain program's by a relative error of at most 0.02.
Values may be sent and summed in bfloat16 or wider, within the bound.
No kernel may reach another device: no remote copies, remote signals or barrier semaphores. Data moves between devices by JAX's collectives and lax.ppermute only.
A program may use at most 192 MiB of HBM per device.

v0:
```python
import jax
import jax.numpy as jnp
from jax import lax
from jax.sharding import PartitionSpec as P

D = 1024
H = 16


EPSILON = 1e-05


def normalize(values, gain, shift):
    center = values - jnp.mean(values, axis=-1, keepdims=True)
    spread = jnp.mean(center * center, axis=-1, keepdims=True)
    return center * lax.rsqrt(spread + EPSILON) * gain + shift


def gelu_tanh(values):
    return jax.nn.gelu(values, approximate=True)


def product(left_side, right_side):
    return jnp.dot(left_side, right_side, preferred_element_type=jnp.float32)


def product_back(left_side, weight_rows):
    return lax.dot_general(
        left_side, weight_rows, (((1,), (1,)), ((), ())), preferred_element_type=jnp.float32
    )


def product_over_rows(left_side, right_side):
    return lax.dot_general(
        left_side, right_side, (((0,), (0,)), ((), ())), preferred_element_type=jnp.float32
    )


def owner_rows(left_side, right_side):
    return lax.psum_scatter(
        product_over_rows(left_side, right_side).astype(jnp.bfloat16),
        "fsdp",
        scatter_dimension=0,
        tiled=True,
    ).astype(jnp.float32)


def attention_scores(query_block, keys_all, doc_ids, slopes, first_row, score_scale):
    block_rows = query_block.shape[0]
    length = keys_all.shape[0]
    query_places = first_row + jnp.arange(block_rows, dtype=jnp.int32)
    key_places = jnp.arange(length, dtype=jnp.int32)
    raw = (
        jnp.einsum("ihd,jhd->hij", query_block, keys_all, preferred_element_type=jnp.float32)
        * score_scale
    )
    distance = (query_places[:, None] - key_places[None, :]).astype(jnp.float32)
    raw = raw - slopes[:, None, None] * distance[None]
    query_docs = lax.dynamic_slice_in_dim(doc_ids, first_row, block_rows, 0)
    allowed = (key_places[None, :] <= query_places[:, None]) & (
        query_docs[:, None] == doc_ids[None, :]
    )
    return (raw, allowed[None])


def body(
    hidden_in,
    segment_ids,
    ln1_gain,
    ln1_bias,
    w_qkv,
    b_qv,
    w_out,
    b_out,
    ln2_gain,
    ln2_bias,
    w_up,
    b_up,
    w_down,
    b_down,
    cotangent,
):
    (
        full_qkv,
        full_out,
        full_up,
        full_down,
        full_bqv,
        full_bout,
        full_bup,
        full_bdown,
        full_gain_one,
        full_shift_one,
        full_gain_two,
        full_shift_two,
    ) = (
        lax.all_gather(w_qkv, "fsdp", axis=0, tiled=True),
        lax.all_gather(w_out, "fsdp", axis=0, tiled=True),
        lax.all_gather(w_up, "fsdp", axis=0, tiled=True),
        lax.all_gather(w_down, "fsdp", axis=0, tiled=True),
        lax.all_gather(b_qv, "fsdp", axis=1, tiled=True),
        lax.all_gather(b_out, "fsdp", axis=0, tiled=True),
        lax.all_gather(b_up, "fsdp", axis=0, tiled=True),
        lax.all_gather(b_down, "fsdp", axis=0, tiled=True),
        lax.all_gather(ln1_gain, "fsdp", axis=0, tiled=True),
        lax.all_gather(ln1_bias, "fsdp", axis=0, tiled=True),
        lax.all_gather(ln2_gain, "fsdp", axis=0, tiled=True),
        lax.all_gather(ln2_bias, "fsdp", axis=0, tiled=True),
    )
    doc_ids = lax.all_gather(segment_ids, "seq", axis=1, tiled=True)[0]
    tokens = hidden_in[0].astype(jnp.float32)
    width = tokens.shape[1]
    length = doc_ids.shape[0]
    gain_one = full_gain_one.astype(jnp.float32)
    shift_one = full_shift_one.astype(jnp.float32)
    gain_two = full_gain_two.astype(jnp.float32)
    shift_two = full_shift_two.astype(jnp.float32)
    normed_low = normalize(tokens, gain_one, shift_one).astype(jnp.bfloat16)
    qkv_bias = jnp.concatenate(
        [
            full_bqv[0].astype(jnp.float32),
            jnp.zeros((width,), jnp.float32),
            full_bqv[1].astype(jnp.float32),
        ]
    )
    projected = (product(normed_low, full_qkv) + qkv_bias).astype(jnp.bfloat16)
    stacked = jnp.stack(
        [projected[:, :width], projected[:, width : 2 * width], projected[:, 2 * width :]]
    )
    by_heads = lax.all_to_all(stacked, "seq", split_axis=2, concat_axis=1, tiled=True)
    local_width = by_heads.shape[2]
    head_size = D // H
    local_heads = local_width // head_size
    queries = by_heads[0].reshape(length, local_heads, head_size)
    keys_all = by_heads[1].reshape(length, local_heads, head_size)
    values_all = by_heads[2].reshape(length, local_heads, head_size)
    first_head = lax.axis_index("seq") * local_heads
    slopes = 2.0 ** (-8.0 * (first_head + jnp.arange(local_heads) + 1).astype(jnp.float32) / H)
    score_scale = head_size ** (-0.5)
    block_rows = min(512, length)
    block_count = length // block_rows

    def forward_block(block_index):
        first_row = block_index * block_rows
        query_block = lax.dynamic_slice_in_dim(queries, first_row, block_rows, 0)
        raw, allowed = attention_scores(
            query_block, keys_all, doc_ids, slopes, first_row, score_scale
        )
        masked = jnp.where(allowed, raw, -1e30)
        highest = jnp.max(masked, axis=-1, keepdims=True)
        weights = jnp.exp(masked - highest)
        total = jnp.sum(weights, axis=-1, keepdims=True)
        probs_low = (weights / total).astype(jnp.bfloat16)
        context = jnp.einsum(
            "hij,jhd->ihd", probs_low, values_all, preferred_element_type=jnp.float32
        )
        return (context.reshape(block_rows, local_width), highest[..., 0] + jnp.log(total[..., 0]))

    contexts, log_totals = lax.map(forward_block, jnp.arange(block_count))
    context_low = contexts.reshape(length, local_width).astype(jnp.bfloat16)
    gathered_context = lax.all_to_all(context_low, "seq", split_axis=0, concat_axis=1, tiled=True)
    first_sum = tokens + product(gathered_context, full_out) + full_bout.astype(jnp.float32)
    normed_two_low = normalize(first_sum, gain_two, shift_two).astype(jnp.bfloat16)
    upward = product(normed_two_low, full_up) + full_bup.astype(jnp.float32)
    activated_low = gelu_tanh(upward).astype(jnp.bfloat16)
    result = first_sum + product(activated_low, full_down) + full_bdown.astype(jnp.float32)
    output = result.astype(jnp.bfloat16)[None]
    back_qkv, back_out, back_up, back_down = (
        lax.all_gather(w_qkv, "fsdp", axis=0, tiled=True),
        lax.all_gather(w_out, "fsdp", axis=0, tiled=True),
        lax.all_gather(w_up, "fsdp", axis=0, tiled=True),
        lax.all_gather(w_down, "fsdp", axis=0, tiled=True),
    )
    grad_branch = cotangent[0]
    grad_top = grad_branch.astype(jnp.float32)
    grad_bdown = jnp.sum(grad_top, axis=0)
    grad_act = product_back(grad_branch, back_down)
    unused_up, gelu_back = jax.vjp(gelu_tanh, upward)
    grad_upward = gelu_back(grad_act)[0].astype(jnp.bfloat16)
    grad_bup = jnp.sum(grad_upward.astype(jnp.float32), axis=0)
    grad_normed_two = product_back(grad_upward, back_up)
    unused_two, norm_back_two = jax.vjp(normalize, first_sum, gain_two, shift_two)
    grad_first_norm, grad_gain_two, grad_shift_two = norm_back_two(grad_normed_two)
    grad_first = grad_top + grad_first_norm
    grad_attended = grad_first.astype(jnp.bfloat16)
    grad_bout = jnp.sum(grad_attended.astype(jnp.float32), axis=0)
    grad_context = product_back(grad_attended, back_out).astype(jnp.bfloat16)
    grad_by_heads = lax.all_to_all(
        grad_context, "seq", split_axis=1, concat_axis=0, tiled=True
    ).reshape(length, local_heads, head_size)

    def backward_block(running, block_index):
        grad_keys, grad_values = running
        first_row = block_index * block_rows
        query_block = lax.dynamic_slice_in_dim(queries, first_row, block_rows, 0)
        grad_block = lax.dynamic_slice_in_dim(grad_by_heads, first_row, block_rows, 0)
        raw, allowed = attention_scores(
            query_block, keys_all, doc_ids, slopes, first_row, score_scale
        )
        probs = jnp.where(allowed, jnp.exp(raw - log_totals[block_index][:, :, None]), 0.0)
        probs_low = probs.astype(jnp.bfloat16)
        grad_values = grad_values + jnp.einsum(
            "hij,ihd->jhd", probs_low, grad_block, preferred_element_type=jnp.float32
        )
        grad_probs = jnp.einsum(
            "ihd,jhd->hij", grad_block, values_all, preferred_element_type=jnp.float32
        )
        grad_scores = (
            probs * (grad_probs - jnp.sum(probs * grad_probs, axis=-1, keepdims=True))
        ).astype(jnp.bfloat16)
        grad_query = (
            jnp.einsum("hij,jhd->ihd", grad_scores, keys_all, preferred_element_type=jnp.float32)
            * score_scale
        )
        grad_keys = (
            grad_keys
            + jnp.einsum(
                "hij,ihd->jhd", grad_scores, query_block, preferred_element_type=jnp.float32
            )
            * score_scale
        )
        return ((grad_keys, grad_values), grad_query.reshape(block_rows, local_width))

    zero_state = jnp.zeros((length, local_heads, head_size), jnp.float32)
    (grad_keys, grad_values), grad_queries = lax.scan(
        backward_block, (zero_state, zero_state), jnp.arange(block_count)
    )
    grad_stack = jnp.stack(
        [
            grad_queries.reshape(length, local_width),
            grad_keys.reshape(length, local_width),
            grad_values.reshape(length, local_width),
        ]
    ).astype(jnp.bfloat16)
    grad_parts = lax.all_to_all(grad_stack, "seq", split_axis=1, concat_axis=2, tiled=True)
    grad_projected = jnp.concatenate([grad_parts[0], grad_parts[1], grad_parts[2]], axis=1)
    grad_bqv = jnp.stack(
        [
            jnp.sum(grad_parts[0].astype(jnp.float32), axis=0),
            jnp.sum(grad_parts[2].astype(jnp.float32), axis=0),
        ]
    )
    grad_normed = product_back(grad_projected, back_qkv)
    unused_one, norm_back_one = jax.vjp(normalize, tokens, gain_one, shift_one)
    grad_tokens_norm, grad_gain_one, grad_shift_one = norm_back_one(grad_normed)
    grad_input = (grad_first + grad_tokens_norm).astype(jnp.bfloat16)[None]
    (
        own_gain_one,
        own_shift_one,
        own_bqv,
        own_bout,
        own_gain_two,
        own_shift_two,
        own_bup,
        own_bdown,
    ) = (
        lax.psum_scatter(
            grad_gain_one.astype(jnp.bfloat16), "fsdp", scatter_dimension=0, tiled=True
        ).astype(jnp.float32),
        lax.psum_scatter(
            grad_shift_one.astype(jnp.bfloat16), "fsdp", scatter_dimension=0, tiled=True
        ).astype(jnp.float32),
        lax.psum_scatter(
            grad_bqv.astype(jnp.bfloat16), "fsdp", scatter_dimension=1, tiled=True
        ).astype(jnp.float32),
        lax.psum_scatter(
            grad_bout.astype(jnp.bfloat16), "fsdp", scatter_dimension=0, tiled=True
        ).astype(jnp.float32),
        lax.psum_scatter(
            grad_gain_two.astype(jnp.bfloat16), "fsdp", scatter_dimension=0, tiled=True
        ).astype(jnp.float32),
        lax.psum_scatter(
            grad_shift_two.astype(jnp.bfloat16), "fsdp", scatter_dimension=0, tiled=True
        ).astype(jnp.float32),
        lax.psum_scatter(
            grad_bup.astype(jnp.bfloat16), "fsdp", scatter_dimension=0, tiled=True
        ).astype(jnp.float32),
        lax.psum_scatter(
            grad_bdown.astype(jnp.bfloat16), "fsdp", scatter_dimension=0, tiled=True
        ).astype(jnp.float32),
    )
    part_qkv = owner_rows(normed_low, grad_projected)
    part_out = owner_rows(gathered_context, grad_attended)
    part_up = owner_rows(normed_two_low, grad_upward)
    part_down = owner_rows(activated_low, grad_branch)
    (
        sum_qkv,
        sum_out,
        sum_up,
        sum_down,
        sum_gain_one,
        sum_shift_one,
        sum_bqv,
        sum_bout,
        sum_gain_two,
        sum_shift_two,
        sum_bup,
        sum_bdown,
    ) = (
        lax.psum(part_qkv.astype(jnp.bfloat16), "seq").astype(jnp.float32),
        lax.psum(part_out.astype(jnp.bfloat16), "seq").astype(jnp.float32),
        lax.psum(part_up.astype(jnp.bfloat16), "seq").astype(jnp.float32),
        lax.psum(part_down.astype(jnp.bfloat16), "seq").astype(jnp.float32),
        lax.psum(own_gain_one.astype(jnp.bfloat16), "seq").astype(jnp.float32),
        lax.psum(own_shift_one.astype(jnp.bfloat16), "seq").astype(jnp.float32),
        lax.psum(own_bqv.astype(jnp.bfloat16), "seq").astype(jnp.float32),
        lax.psum(own_bout.astype(jnp.bfloat16), "seq").astype(jnp.float32),
        lax.psum(own_gain_two.astype(jnp.bfloat16), "seq").astype(jnp.float32),
        lax.psum(own_shift_two.astype(jnp.bfloat16), "seq").astype(jnp.float32),
        lax.psum(own_bup.astype(jnp.bfloat16), "seq").astype(jnp.float32),
        lax.psum(own_bdown.astype(jnp.bfloat16), "seq").astype(jnp.float32),
    )
    return (
        output,
        grad_input,
        sum_gain_one,
        sum_shift_one,
        sum_qkv,
        sum_bqv,
        sum_out,
        sum_bout,
        sum_gain_two,
        sum_shift_two,
        sum_up,
        sum_bup,
        sum_down,
        sum_bdown,
    )


def solution(mesh):
    return jax.shard_map(
        body,
        mesh=mesh,
        in_specs=(
            P("fsdp", "seq", None),
            P("fsdp", "seq"),
            P("fsdp"),
            P("fsdp"),
            P("fsdp", None),
            P(None, "fsdp"),
            P("fsdp", None),
            P("fsdp"),
            P("fsdp"),
            P("fsdp"),
            P("fsdp", None),
            P("fsdp"),
            P("fsdp", None),
            P("fsdp"),
            P("fsdp", "seq", None),
        ),
        out_specs=(
            P("fsdp", "seq", None),
            P("fsdp", "seq", None),
            P("fsdp"),
            P("fsdp"),
            P("fsdp", None),
            P(None, "fsdp"),
            P("fsdp", None),
            P("fsdp"),
            P("fsdp"),
            P("fsdp"),
            P("fsdp", None),
            P("fsdp"),
            P("fsdp", None),
            P("fsdp"),
        ),
        check_vma=False,
    )
```

profile of v0, /device:TPU:8, one launch (start us, length us, event | category | flops | bytes accessed | tf_op | source)
XLA Modules:
  0.0 787.9 jit_solution(1537978671429891288)
XLA Ops:
  10.0 9.1 %all-gather.1 = bf16[8,1,128]{2,1,0:T(2,128)(2,1)S(1)} all-gather(bf16[1,1,128]{2,1,0:T(2,128)(2,1)} %bitcast.240), channel_id=1, replica_groups=mesh['seq'=4,'fsdp'=8] {'fsdp'}, dimensions={0}, use_global_device_ids=true | all-gather | bytes 2304 | tf_op jit(solution)/shard_map/all_gather | solution.py:106
  19.1 11.9 %all-gather = bf16[8,1,128]{2,1,0:T(2,128)(2,1)S(1)} all-gather(bf16[1,1,128]{2,1,0:T(2,128)(2,1)} %bitcast.241), channel_id=1, replica_groups=mesh['seq'=4,'fsdp'=8] {'fsdp'}, dimensions={0}, use_global_device_ids=true | all-gather | bytes 2304 | tf_op jit(solution)/shard_map/all_gather | solution.py:105
  31.0 9.1 %all_gather.47 = bf16[2,1024]{1,0:T(2,128)(2,1)S(1)} all-gather(bf16[2,128]{1,0:T(2,128)(2,1)} %param.24), channel_id=1, replica_groups=mesh['seq'=4,'fsdp'=8] {'fsdp'}, dimensions={1}, use_global_device_ids=true | all-gather | bytes 4608 | tf_op jit(solution)/shard_map/all_gather | solution.py:101
  42.7 30.7 %all-gather.12.cloned.1.call-done = bf16[1024,3072]{1,0:T(8,128)(2,1)} async-done(((bf16[128,3072]{1,0:T(8,128)(2,1)}), bf16[1024,3072]{1,0:T(8,128)(2,1)}) %all-gather.12.cloned.1.call-update) | async-done | bytes 6291472 | tf_op jit(solution)/shard_map/all_gather | solution.py:97
  84.7 27.0 %all_gather.43 = s32[1,1024]{1,0:T(1,128)S(1)} all-gather(s32[1,256]{1,0:T(1,128)S(1)} %copy-done.39), channel_id=1, replica_groups=mesh['seq'=4,'fsdp'=8] {'seq'}, dimensions={1}, use_global_device_ids=true | all-gather | bytes 5120 | tf_op jit(solution)/shard_map/all_gather | solution.py:110
  121.8 28.4 %while.28 = (s32[]{:T(128)}, bf16[2,512,256]{2,1,0:T(8,128)(2,1)}, f32[2,4,512]{2,1,0:T(4,128)S(1)}, s32[2]{0:T(128)S(1)}, s32[1024]{0:T(1024)S(1)}, /*index=5*/...) while((s32[]{:T(128)}, bf16[2,512,256]{2,1,0:T(8,128)(2,1)}, ...), condition=%wide.region_5.6_spmd.clone, body=%wide.region_2.5_spmd.clone.sunk | while | flops 577239552 | bytes 38355232 | solution.py:159
  154.4 11.3 %all-gather.2 = bf16[8,1,128]{2,1,0:T(2,128)(2,1)S(1)} all-gather(bf16[1,1,128]{2,1,0:T(2,128)(2,1)S(1)} %bitcast.242), channel_id=1, replica_groups=mesh['seq'=4,'fsdp'=8] {'fsdp'}, dimensions={0}, use_global_device_ids=true | all-gather | bytes 2304 | tf_op jit(solution)/shard_map/all_gather | solution.py:102
  165.7 11.5 %all-gather.5 = bf16[8,1,512]{2,1,0:T(2,128)(2,1)S(1)} all-gather(bf16[1,1,512]{2,1,0:T(2,128)(2,1)S(1)} %reshape.315), channel_id=1, replica_groups=mesh['seq'=4,'fsdp'=8] {'fsdp'}, dimensions={0}, use_global_device_ids=true | all-gather | bytes 9216 | tf_op jit(solution)/shard_map/all_gather | solution.py:103
  177.3 10.4 %all-gather.4 = bf16[8,1,128]{2,1,0:T(2,128)(2,1)S(1)} all-gather(bf16[1,1,128]{2,1,0:T(2,128)(2,1)S(1)} %bitcast.243), channel_id=1, replica_groups=mesh['seq'=4,'fsdp'=8] {'fsdp'}, dimensions={0}, use_global_device_ids=true | all-gather | bytes 2304 | tf_op jit(solution)/shard_map/all_gather | solution.py:108
  187.7 9.0 %all-gather.3 = bf16[8,1,128]{2,1,0:T(2,128)(2,1)S(1)} all-gather(bf16[1,1,128]{2,1,0:T(2,128)(2,1)S(1)} %bitcast.244), channel_id=1, replica_groups=mesh['seq'=4,'fsdp'=8] {'fsdp'}, dimensions={0}, use_global_device_ids=true | all-gather | bytes 2304 | tf_op jit(solution)/shard_map/all_gather | solution.py:107
  200.0 7.9 %convolution_add_fusion = f32[256,4096]{1,0:T(8,128)} fusion(bf16[1024,4096]{1,0:T(8,128)(2,1)} %all-gather.16.cloned.1.call-done, f32[4096]{0:T(1024)S(1)} %bitcast.232, f32[256,1024]{1,0:T(8,128)S(1)} %get-tuple-element.316, f32[1024]{0:T(1024)S(1)} %bitcast.221, f32[1024]{0:T(1024)S(1)} %bitcast.217, f32[256]{0:T(256)S(1)} %fusion.66, ...), kind=kOutput, calls=%fused_computation.52 | convolution fusion | flops 2149842944 | bytes 13658112 | tf_op jit(solution)/shard_map/dot_general | solution.py:24
  207.8 60.0 %all-gather.18.cloned.1.call-done = bf16[4096,1024]{1,0:T(8,128)(2,1)} async-done(((bf16[512,1024]{1,0:T(8,128)(2,1)}), bf16[4096,1024]{1,0:T(8,128)(2,1)}) %all-gather.18.cloned.1.call-update) | async-done | bytes 8388624 | tf_op jit(solution)/shard_map/all_gather | solution.py:100
  267.8 12.1 %fusion.78 = (bf16[4096]{0:T(1024)(128)(2,1)}, bf16[256,4096]{1,0:T(8,128)(2,1)S(1)}) fusion(f32[256,4096]{1,0:T(8,128)} %convolution_add_fusion, bf16[4096,1024]{1,0:T(8,128)(2,1)} %all-gather.18.cloned.1.call-done, bf16[1,256,1024]{2,1,0:T(8,128)(2,1)S(1)} %copy-done.9), kind=kOutput, calls=%fused_computation.130 | convolution fusion | flops 2169499648 | bytes 15212544 | tf_op jit(solution)/shard_map/dot_general | solution.py:28
  303.2 60.3 %while.29 = (s32[]{:T(128)}, f32[1024,4,64]{0,2,1:T(8,128)S(1)}, f32[1024,4,64]{0,2,1:T(8,128)S(1)}, bf16[2,512,256]{2,1,0:T(8,128)(2,1)}, s32[2]{0:T(128)S(1)},...) while((s32[]{:T(128)}, f32[1024,4,64]{0,2,1:T(8,128)S(1)}, ...), condition=%wide.region_12.13_spmd.clone, body=%wide.region_10.12_spmd.clone.sunk | while | flops 1369438720 | bytes 185393632 | solution.py:225
  366.1 27.8 %all_to_all.62 = bf16[3,1024,256]{2,0,1:T(4,128)(2,1)S(1)} all-to-all(bf16[3,1024,256]{2,0,1:T(4,128)(2,1)S(1)} %copy.76), channel_id=1, replica_groups=mesh['seq'=4,'fsdp'=8] {'seq'}, dimensions={1} | all-to-all | bytes 3145728 | tf_op jit(solution)/shard_map/all_to_all | solution.py:235
  410.3 8.5 %convolution_convert_fusion = bf16[4096,1024]{1,0:T(8,128)(2,1)} fusion(bf16[1,256,1024]{2,1,0:T(8,128)(2,1)S(1)} %copy-done.10, f32[256,4096]{1,0:T(8,128)} %convolution_add_fusion), kind=kOutput, calls=%fused_computation.47 | convolution fusion | flops 2161115136 | bytes 13107200 | tf_op jit(solution)/shard_map/dot_general | solution.py:34
  419.9 47.6 %reduce-scatter.8.cloned.1.call-done = bf16[128,3072]{1,0:T(8,128)(2,1)} async-done(((bf16[1024,3072]{1,0:T(8,128)(2,1)}), bf16[128,3072]{1,0:T(8,128)(2,1)}) %reduce-scatter.8.cloned.1.call-update) | async-done | bytes 786448 | tf_op jit(solution)/shard_map/reduce_scatter | solution.py:40
  467.5 90.3 %reduce-scatter.12.cloned.1.call-done = bf16[128,4096]{1,0:T(8,128)(2,1)} async-done(((bf16[1024,4096]{1,0:T(8,128)(2,1)}), bf16[128,4096]{1,0:T(8,128)(2,1)}) %reduce-scatter.12.cloned.1.call-update) | async-done | bytes 1048592 | tf_op jit(solution)/shard_map/reduce_scatter | solution.py:40
  557.8 90.3 %reduce-scatter.14.cloned.1.call-done = bf16[512,1024]{1,0:T(8,128)(2,1)} async-done(((bf16[4096,1024]{1,0:T(8,128)(2,1)}), bf16[512,1024]{1,0:T(8,128)(2,1)}) %reduce-scatter.14.cloned.1.call-update) | async-done | bytes 1048592 | tf_op jit(solution)/shard_map/reduce_scatter | solution.py:40
  648.1 12.0 %all-gather.6 = bf16[8,1,128]{2,1,0:T(2,128)(2,1)S(1)} all-gather(bf16[1,1,128]{2,1,0:T(2,128)(2,1)S(1)} %bitcast.245), channel_id=1, replica_groups=mesh['seq'=4,'fsdp'=8] {'fsdp'}, dimensions={0}, use_global_device_ids=true | all-gather | bytes 2304 | tf_op jit(solution)/shard_map/all_gather | solution.py:104
  662.1 8.3 %fusion.49 = bf16[1,256,1024]{2,1,0:T(8,128)(2,1)} fusion(f32[256,1024]{1,0:T(8,128)S(1)} %copy-done.4, bf16[4096,1024]{1,0:T(8,128)(2,1)} %all-gather.18.cloned.1.call-done, f32[1024]{0:T(1024)S(1)} %bitcast.239, f32[256,4096]{1,0:T(8,128)} %convolution_add_fusion), kind=kOutput, calls=%fused_computation.82 | convolution fusion | flops 2157707264 | bytes 14159872 | tf_op jit(solution)/shard_map/dot_general | solution.py:24
  676.0 23.6 %all-reduce.7 = (bf16[1024]{0:T(1024)(128)(2,1)S(1)}, bf16[1024]{0:T(1024)(128)(2,1)S(1)}, bf16[1024]{0:T(1024)(128)(2,1)S(1)}, bf16[1024]{0:T(1024)(128)(2,1)S(...) all-reduce(bf16[1024]{0:T(1024)(128)(2,1)S(1)} %get-tuple-element.2, ...), channel_id=2, replica_groups=mesh['seq'=4,'fsdp'=8] {'fsdp'}, use_global_device_ids=true, to_apply=%region_16.17.clone | all-reduce | flops 10240 | bytes 40960
  702.3 10.0 %all-reduce.8 = (bf16[128]{0:T(256)(128)(2,1)S(1)}, bf16[128]{0:T(256)(128)(2,1)S(1)}, bf16[2,128]{1,0:T(2,128)(2,1)S(1)}, bf16[128]{0:T(256)(128)(2,1)S(1)}, bf...) all-reduce(bf16[128]{0:T(256)(128)(2,1)S(1)} %dynamic-slice.1, ...), channel_id=1, replica_groups=mesh['seq'=4,'fsdp'=8] {'seq'}, use_global_device_ids=true, to_apply=%region_17.18 | all-reduce | flops 1536 | bytes 6144 | tf_op jit(solution)/shard_map/psum | solution.py:304
  716.5 55.7 %all-reduce.12.cloned.1.call-done = (bf16[128,3072]{1,0:T(8,128)(2,1)}, bf16[128,1024]{1,0:T(8,128)(2,1)}, bf16[128,4096]{1,0:T(8,128)(2,1)}, bf16[512,1024]{1,0:T(8,128)(2,1)}) async-done(((bf16[128,3072]{1,0:T(8,128)(2,1)}, bf16[128,1024]{1,0:T(8,128)(2,1)}, bf16[128,4096]{1,0:T(8,128)(2,1)}, bf16[512,1024]{1,0:T(8,128)(2,1)}), (bf16[128,3072]{1,0:T(8,128)(2,1)}, bf16[128,1024]{1,0:T(8,128)(2,1)}, ...) | async-done | bytes 3145744 | tf_op jit(solution)/shard_map/psum | solution.py:300
  (286 shorter events, 180.6 us)
Async XLA Ops:
  7.2 66.2 %copy-start.5 = (bf16[1,256,1024]{2,1,0:T(8,128)(2,1)S(1)}, bf16[1,256,1024]{2,1,0:T(8,128)(2,1)}, u32[]{:S(2)}) copy-start(bf16[1,256,1024]{2,1,0:T(8,128)(2,1)} %param.19) | copy-start | bytes 1572868
  7.2 66.2 %all-gather.12.cloned.1.call-start = ((), (), s32[]{:S(2)}) async-start(), calls=%async_computation.9 | async-start | bytes 7077888 | tf_op jit(solution)/shard_map/all_gather | solution.py:97
  7.9 189.0 %all-gather.14.cloned.1.call-start = ((), (), s32[]{:S(2)}) async-start(), calls=%async_computation.10 | async-start | bytes 2359296 | tf_op jit(solution)/shard_map/all_gather | solution.py:98
  8.7 191.3 %all-gather.16.cloned.1.call-start = ((), (), s32[]{:S(2)}) async-start(), calls=%async_computation.11 | async-start | bytes 9437184 | tf_op jit(solution)/shard_map/all_gather | solution.py:99
  9.4 258.4 %all-gather.18.cloned.1.call-start = ((), (), s32[]{:S(2)}) async-start(), calls=%async_computation.12 | async-start | bytes 9437184 | tf_op jit(solution)/shard_map/all_gather | solution.py:100
  19.1 59.0 %copy-start.35 = (f32[8,1,128]{2,1,0:T(1,128)}, f32[8,1,128]{2,1,0:T(1,128)S(1)}, u32[]{:S(2)}) copy-start(f32[8,1,128]{2,1,0:T(1,128)S(1)} %convert_element_type.252) | copy-start | bytes 12292
  31.0 47.1 %copy-start.23 = (f32[8,1,128]{2,1,0:T(1,128)}, f32[8,1,128]{2,1,0:T(1,128)S(1)}, u32[]{:S(2)}) copy-start(f32[8,1,128]{2,1,0:T(1,128)S(1)} %convert_element_type.251) | copy-start | bytes 12292
  41.3 36.8 %copy-start.25 = (f32[256]{0:T(256)}, f32[256]{0:T(256)S(1)}, u32[]{:S(2)}) copy-start(f32[256]{0:T(256)S(1)} %broadcast_multiply_fusion.1) | copy-start | bytes 3076
  81.0 30.7 %all-to-all-start = ((bf16[3,256,1024]{1,0,2:T(4,128)(2,1)}), bf16[3,256,1024]{1,0,2:T(4,128)(2,1)S(1)}, u32[]{:S(2)}, u32[]{:S(2)}) async-start(bf16[3,256,1024]{1,0,2:T(4,128)(2,1)} %copy.65), calls=%async_computation | async-start | bytes 4194304 | tf_op jit(solution)/shard_map/all_to_all | solution.py:130
  121.8 44.0 %copy-start.40 = (bf16[512]{0:T(512)(128)(2,1)S(1)}, bf16[512]{0:T(512)(128)(2,1)}, u32[]{:S(2)}) copy-start(bf16[512]{0:T(512)(128)(2,1)} %param.30) | copy-start | bytes 3076
  121.8 55.5 %copy-start.42 = (bf16[128]{0:T(256)(128)(2,1)S(1)}, bf16[128]{0:T(256)(128)(2,1)}, u32[]{:S(2)}) copy-start(bf16[128]{0:T(256)(128)(2,1)} %param.28) | copy-start | bytes 772
  121.8 65.9 %copy-start.43 = (bf16[128]{0:T(256)(128)(2,1)S(1)}, bf16[128]{0:T(256)(128)(2,1)}, u32[]{:S(2)}) copy-start(bf16[128]{0:T(256)(128)(2,1)} %param.27) | copy-start | bytes 772
  150.2 46.6 %all-to-all-start.1 = ((bf16[4,256,256]{2,1,0:T(8,128)(2,1)}), bf16[4,256,256]{2,1,0:T(8,128)(2,1)S(1)}, u32[]{:S(2)}, u32[]{:S(2)}) async-start(bf16[4,256,256]{2,1,0:T(8,128)(2,1)} %bitcast.199), calls=%async_computation.1 | async-start | bytes 1048576 | tf_op jit(solution)/shard_map/all_to_all | solution.py:161
  199.6 83.5 %copy-start.3 = (f32[256,1024]{1,0:T(8,128)}, f32[256,1024]{1,0:T(8,128)S(1)}, u32[]{:S(2)}) copy-start(f32[256,1024]{1,0:T(8,128)S(1)} %get-tuple-element.316) | copy-start | bytes 3145732
  200.0 67.9 %copy-start.9 = (bf16[1,256,1024]{2,1,0:T(8,128)(2,1)S(1)}, bf16[1,256,1024]{2,1,0:T(8,128)(2,1)}, u32[]{:S(2)}) copy-start(bf16[1,256,1024]{2,1,0:T(8,128)(2,1)} %param.33) | copy-start | bytes 1572868
  286.9 12.9 %all-to-all-start.2 = ((bf16[256,4,256]{2,0,1:T(8,128)(2,1)}), bf16[256,4,256]{2,0,1:T(8,128)(2,1)}, u32[]{:S(2)}, u32[]{:S(2)}) async-start(bf16[256,4,256]{2,0,1:T(8,128)(2,1)} %bitcast.153), calls=%async_computation.2 | async-start | bytes 1048576 | tf_op jit(solution)/shard_map/all_to_all | solution.py:188
  291.1 128.9 %reduce-scatter.10.cloned.1.call-start = ((), (), s32[]{:S(2)}) async-start(), calls=%async_computation.14 | async-start | bytes 2359296 | tf_op jit(solution)/shard_map/reduce_scatter | solution.py:40
  294.2 173.3 %reduce-scatter.8.cloned.1.call-start = ((), (), s32[]{:S(2)}) async-start(), calls=%async_computation.13 | async-start | bytes 7077888 | tf_op jit(solution)/shard_map/reduce_scatter | solution.py:40
  400.7 157.1 %reduce-scatter.12.cloned.1.call-start = ((), (), s32[]{:S(2)}) async-start(), calls=%async_computation.15 | async-start | bytes 9437184 | tf_op jit(solution)/shard_map/reduce_scatter | solution.py:40
  409.3 238.8 %reduce-scatter.14.cloned.1.call-start = ((), (), s32[]{:S(2)}) async-start(), calls=%async_computation.16 | async-start | bytes 9437184 | tf_op jit(solution)/shard_map/reduce_scatter | solution.py:40
  418.8 229.3 %copy-start.44 = (bf16[128]{0:T(256)(128)(2,1)S(1)}, bf16[128]{0:T(256)(128)(2,1)}, u32[]{:S(2)}) copy-start(bf16[128]{0:T(256)(128)(2,1)} %param.32) | copy-start | bytes 772
  418.9 241.3 %copy-start.46 = (u32[32]{0:T(128)S(1)}, u32[32]{0:T(128)}, u32[]{:S(2)}) copy-start(u32[32]{0:T(128)} %constant.102) | copy-start | bytes 388
  418.9 282.6 %reduce-scatter.16.cloned.1.call-start = ((), (), s32[]{:S(2)}) async-start(), calls=%async_computation.17 | async-start | bytes 294912
  419.9 352.3 %all-reduce.12.cloned.1.call-start = ((), (), s32[]{:S(2)}) async-start(), calls=%async_computation.18 | async-start | bytes 6291456 | tf_op jit(solution)/shard_map/psum | solution.py:300
  (43 other events, 343.8 us)
Sparse Core Ops, SparseCore 0:
  9.7 63.6 all-gather.11
  75.0 29.9 all-gather.13
  106.6 79.0 all-gather.15
  187.2 80.5 all-gather.17
  294.5 33.6 reduce-scatter.9
  400.8 66.6 reduce-scatter.7
  469.8 87.9 reduce-scatter.11
  560.1 87.9 reduce-scatter.13
  650.9 28.0 reduce-scatter.15
  682.5 89.6 all-reduce.11
where the time goes:
time: 794 us; the launch traced here: 788 us
  waiting for transfers between devices  382 us (48%)
  blocking collectives  173 us (22%)
  matrix products  123 us (15%)
  local copies, waits for them, and re-layouts  39.6 us (5%)
  other arithmetic  34 us (4%)
  between operations  16.4 us (2%)
  starting transfers between devices  13 us (2%)
    reduce_scatter x4, waiting for transfers between devices, owner_rows(): lax.psum_scatter(product_over_rows(left_side, right_side).astype(jnp.bflo...  228 us
    all_gather x1, waiting for transfers between devices, body(): lax.all_gather(w_down, 'fsdp', axis=0, tiled=True)  60 us
    psum x1, waiting for transfers between devices, body(): lax.psum(part_qkv.astype(jnp.bfloat16), 'seq').astype(jnp.float32)  55.7 us
    all_gather x1, waiting for transfers between devices, body(): lax.all_gather(w_qkv, 'fsdp', axis=0, tiled=True)  30.7 us
    all_to_all x1, blocking collectives, body(): lax.all_to_all(grad_stack, 'seq', split_axis=1, concat_axis=2, tiled=True)  27.8 us
    all_gather x1, blocking collectives, body(): doc_ids = lax.all_gather(segment_ids, 'seq', axis=1, tiled=True)[0]  27 us
    dot_general x4, matrix products, product_over_rows(): lax.dot_general(left_side, right_side, (((0,), (0,)), ((), ())), preferre...  23.8 us
    unnamed x1, blocking collectives  23.6 us
  transfers between devices with their start and end apart: 13, of which 7 were waited for; matrix products, arithmetic and copies ran while one was open for 20% of the time, Pallas kernels for 0%

commit v1 on v0

v1 whole, which is shorter than its diff:
```python
import functools

import jax
import jax.numpy as jnp
from jax import lax
from jax.experimental import pallas as pl
from jax.experimental.pallas import tpu as pltpu
from jax.sharding import PartitionSpec as P

D = 1024
H = 16
HEAD = D // H
EPSILON = 1e-05
F32 = jnp.float32
BF16 = jnp.bfloat16
NT = (((1,), (1,)), ((), ()))
NN = (((1,), (0,)), ((), ()))
TN = (((0,), (0,)), ((), ()))


def dot(a, b, dims=NN):
    return lax.dot_general(a, b, dims, preferred_element_type=F32)


def key_start(first_query, block, longest):
    return max(0, (first_query - longest + 1) // block * block)


def masked_distance(seg_col, seg_row, k0, nk, q0, bq):
    key_at = lax.broadcasted_iota(jnp.int32, (nk, bq), 0) + k0
    query_at = lax.broadcasted_iota(jnp.int32, (nk, bq), 1) + q0
    ok = (key_at <= query_at) & (seg_col[k0 : k0 + nk, :] == seg_row[:, q0 : q0 + bq])
    return jnp.where(ok, (query_at - key_at).astype(F32), 1e32)


def only_head(values, head):
    lane = lax.broadcasted_iota(jnp.int32, values.shape, 1)
    return jnp.where(lane // HEAD == head, values, jnp.zeros_like(values))


def attention_kernel(slopes, proj, seg_col, seg_row, context, log_total, *, block, longest):
    length = proj.shape[0]
    width = proj.shape[1] // 3
    for q0 in range(0, length, block):
        k0 = key_start(q0, block, longest)
        nk = q0 + block - k0
        far = masked_distance(seg_col, seg_row, k0, nk, q0, block)
        queries = proj[q0 : q0 + block, :width] * BF16(HEAD**-0.5)
        keys = proj[k0 : k0 + nk, width : 2 * width]
        values = proj[k0 : k0 + nk, 2 * width :].T
        parts = []
        for head in range(width // HEAD):
            raw = dot(keys, only_head(queries, head), NT) - slopes[head] * far
            highest = jnp.max(raw, axis=0, keepdims=True)
            weights = jnp.exp(raw - highest)
            total = jnp.sum(weights, axis=0, keepdims=True)
            probs = (weights * (1.0 / total)).astype(BF16)
            log_total[head : head + 1, q0 : q0 + block] = highest + jnp.log(total)
            parts.append(dot(values[head * HEAD : (head + 1) * HEAD, :], probs))
        context[q0 : q0 + block, :] = jnp.concatenate(parts, axis=0).T.astype(BF16)


def attention_back_kernel(
    slopes, proj, grad, seg_col, seg_row, log_total, out, probs_all, scores_all, grad_keys, grad_values, *, block, longest
):
    length = proj.shape[0]
    width = proj.shape[1] // 3
    heads = width // HEAD
    grad_keys[...] = jnp.zeros_like(grad_keys)
    grad_values[...] = jnp.zeros_like(grad_values)
    for q0 in range(0, length, block):
        k0 = key_start(q0, block, longest)
        nk = q0 + block - k0
        far = masked_distance(seg_col, seg_row, k0, nk, q0, block)
        queries = proj[q0 : q0 + block, :width] * BF16(HEAD**-0.5)
        keys = proj[k0 : k0 + nk, width : 2 * width]
        values = proj[k0 : k0 + nk, 2 * width :]
        keys_t = keys.T
        tops = grad[q0 : q0 + block, :]
        parts, query_rows, top_rows = [], [], []
        for head in range(heads):
            query_head = only_head(queries, head)
            top_head = only_head(tops, head)
            query_rows.append(query_head)
            top_rows.append(top_head)
            raw = dot(keys, query_head, NT) - slopes[head] * far
            probs = jnp.exp(raw - log_total[head : head + 1, q0 : q0 + block])
            probs_all[:nk, head * block : (head + 1) * block] = probs.astype(BF16)
            grad_probs = dot(values, top_head, NT)
            row_sum = jnp.sum(probs * grad_probs, axis=0, keepdims=True)
            scores = (probs * (grad_probs - row_sum)).astype(BF16)
            scores_all[:nk, head * block : (head + 1) * block] = scores
            parts.append(dot(keys_t[head * HEAD : (head + 1) * HEAD, :], scores))
        grad_values[k0 : k0 + nk, :] += dot(probs_all[:nk, :], jnp.concatenate(top_rows, axis=0))
        grad_keys[k0 : k0 + nk, :] += dot(scores_all[:nk, :], jnp.concatenate(query_rows, axis=0))
        out[q0 : q0 + block, :width] = (jnp.concatenate(parts, axis=0).T * HEAD**-0.5).astype(BF16)
    out[:, width : 2 * width] = grad_keys[...].astype(BF16)
    out[:, 2 * width :] = grad_values[...].astype(BF16)


VMEM = pl.BlockSpec(memory_space=pltpu.VMEM)
SMEM = pl.BlockSpec(memory_space=pltpu.SMEM)


def attention(slopes, proj, seg_col, seg_row):
    length, wide = proj.shape
    width = wide // 3
    heads = width // HEAD
    return pl.pallas_call(
        functools.partial(attention_kernel, block=min(256, length), longest=length // 2),
        out_shape=(
            jax.ShapeDtypeStruct((length, width), BF16),
            jax.ShapeDtypeStruct((heads, length), F32),
        ),
        in_specs=[SMEM, VMEM, VMEM, VMEM],
        out_specs=(VMEM, VMEM),
        compiler_params=pltpu.CompilerParams(vmem_limit_bytes=40 * 2**20),
        cost_estimate=pl.CostEstimate(
            flops=3 * length * length * heads * HEAD, bytes_accessed=4 * length * wide, transcendentals=length * length * heads // 2
        ),
        name="attention",
    )(slopes, proj, seg_col, seg_row)


def attention_back(slopes, proj, grad, seg_col, seg_row, log_total):
    length, wide = proj.shape
    width = wide // 3
    heads = width // HEAD
    block = min(256, length)
    most = min(length, block + length // 2)
    return pl.pallas_call(
        functools.partial(attention_back_kernel, block=block, longest=length // 2),
        out_shape=jax.ShapeDtypeStruct((length, wide), BF16),
        in_specs=[SMEM, VMEM, VMEM, VMEM, VMEM, VMEM],
        out_specs=VMEM,
        scratch_shapes=[
            pltpu.VMEM((most, heads * block), BF16),
            pltpu.VMEM((most, heads * block), BF16),
            pltpu.VMEM((length, width), F32),
            pltpu.VMEM((length, width), F32),
        ],
        compiler_params=pltpu.CompilerParams(vmem_limit_bytes=40 * 2**20),
        cost_estimate=pl.CostEstimate(
            flops=8 * length * length * heads * HEAD, bytes_accessed=6 * length * wide, transcendentals=length * length * heads // 2
        ),
        name="attention_back",
    )(slopes, proj, grad, seg_col, seg_row, log_total)


def copy_kernel(plan, inputs, position, *refs):
    for source, target in plan(position, refs[:inputs], refs[inputs:]):
        target[...] = source[...]


def copy_call(name, plan, position, operands, shapes):
    return pl.pallas_call(
        functools.partial(copy_kernel, plan, len(operands)),
        out_shape=tuple(jax.ShapeDtypeStruct(shape, BF16) for shape in shapes),
        in_specs=[SMEM] + [VMEM] * len(operands),
        out_specs=tuple(VMEM for shape in shapes),
        compiler_params=pltpu.CompilerParams(vmem_limit_bytes=40 * 2**20),
        cost_estimate=pl.CostEstimate(flops=0, bytes_accessed=4 * sum(o.size for o in operands), transcendentals=0),
        name=name,
    )(position, *operands)


def widen_columns_kernel(position, *refs, blocks, rows):
    pieces, out = refs[:-2], refs[-2]
    s = position[0]
    count = len(pieces)
    width = pieces[0].shape[1] // blocks
    for k, piece in enumerate(pieces):
        for j in range(blocks):
            at = pl.multiple_of((j * count + (s ^ k)) * width, width)
            out[:, pl.ds(at, width)] = piece[:rows, j * width : (j + 1) * width].astype(F32)
    refs[-1][...] = tree_sum([piece[rows:, :].astype(F32) for piece in pieces])


def widen_feed_kernel(position, *refs, up_rows, blocks):
    pieces, up, down = refs[:-2], refs[-2], refs[-1]
    s = position[0]
    count = len(pieces)
    width = up.shape[1] // (blocks * count)
    own = down.shape[0] // count
    for k, piece in enumerate(pieces):
        for j in range(blocks):
            at = pl.multiple_of((j * count + (s ^ k)) * width, width)
            up[:, pl.ds(at, width)] = piece[:up_rows, j * width : (j + 1) * width].astype(F32)
        down[pl.ds(pl.multiple_of((s ^ k) * own, own), own), :] = piece[up_rows:, :].astype(F32)


def stats(values):
    center = values - jnp.mean(values, axis=-1, keepdims=True)
    spread = jnp.mean(center * center, axis=-1, keepdims=True)
    rate = lax.rsqrt(spread + EPSILON)
    return center * rate, rate


def norm_back(grad, xhat, rate, gain):
    a = grad * gain
    return rate * (
        a - jnp.mean(a, axis=-1, keepdims=True) - xhat * jnp.mean(a * xhat, axis=-1, keepdims=True)
    )


def tree_sum(terms):
    while len(terms) > 1:
        terms = [a + b for a, b in zip(terms[::2], terms[1::2])]
    return terms[0]


def after(value, *others):
    return lax.optimization_barrier((value, *others))[0]


def body(
    seq_size,
    fsdp_size,
    hidden_in,
    segment_ids,
    ln1_gain,
    ln1_bias,
    w_qkv,
    b_qv,
    w_out,
    b_out,
    ln2_gain,
    ln2_bias,
    w_up,
    b_up,
    w_down,
    b_down,
    cotangent,
):
    S, F, Z = seq_size, fsdp_size, fsdp_size // 2
    s = lax.axis_index("seq")
    f = lax.axis_index("fsdp")
    z, core = f // 2, f % 2

    def seq_x(x, k):
        return lax.ppermute(x, "seq", [(i, i ^ k) for i in range(S)])

    def fsdp_x(x, k):
        return lax.ppermute(x, "fsdp", [(i, i ^ k) for i in range(F)])

    def put(buf, value, *index):
        index = tuple(index) + (0,) * (buf.ndim - len(index))
        return lax.dynamic_update_slice(buf, value, index)

    def spread_fsdp(piece):
        own = [piece] + [fsdp_x(piece, 2 * k) for k in range(1, Z)]
        return own, fsdp_x(jnp.stack(own), 1)

    def join_fsdp(name, pair, heights):
        own, other = pair
        columns = own[0].shape[1]
        ends = [sum(heights[: i + 1]) for i in range(len(heights))]

        def plan(position, ins, outs):
            for k in range(Z):
                for source, place in ((ins[k], 2 * k), (ins[Z].at[k], 2 * k + 1)):
                    for end, height, out in zip(ends, heights, outs):
                        yield source.at[end - height : end, :], out.at[position[1] ^ place]

        return copy_call(
            name, plan, place_now, own + [other], [(F, h, columns) for h in heights]
        )

    def gather_seq_parts(x):
        return [x] + [seq_x(x, k) for k in range(1, S)]

    def exchange_seq(x):
        return lax.all_to_all(x, "seq", 0, 0)

    def reduce_fsdp(partials):
        def half(index):
            return jnp.concatenate(
                [
                    lax.dynamic_index_in_dim(p.reshape(Z, 2, *p.shape[1:]), index, 1, keepdims=False)
                    for p in partials
                ],
                axis=1,
            )

        other = fsdp_x(half(1 - core), 1)
        kept = half(core)

        def block(index):
            return lax.dynamic_index_in_dim(kept, index, 0, keepdims=False).astype(
                F32
            ) + lax.dynamic_index_in_dim(other, index, 0, keepdims=False).astype(F32)

        sent = [fsdp_x(block(z ^ k).astype(BF16), 2 * k) for k in range(1, Z)]
        return sum([x.astype(F32) for x in sent], block(z))

    own_rows = hidden_in.shape[1]
    length = own_rows * S
    width = D // S
    heads = width // HEAD
    part = D // F
    ff_part = b_up.shape[0]
    ff_own = ff_part // S
    hidden = hidden_in[0]
    top = cotangent[0]

    place_now = jnp.stack([s, f])
    wide = 3 * width
    small = jnp.concatenate(
        [ln1_gain, ln1_bias, b_qv[0], b_qv[1], b_out, ln2_gain, ln2_bias, b_down, b_up]
    )
    small_size = small.shape[0]
    extra = -(-small_size // (16 * wide)) * 16
    small_rows = jnp.pad(small, (0, extra * wide - small_size)).reshape(extra, wide)

    aligned = ff_own % 128 == 0
    up_source = w_up
    if not aligned:
        up_source = lax.dynamic_index_in_dim(
            w_up.reshape(part, F, S, ff_own), s, 2, keepdims=False
        ).reshape(ff_own, D)

    def pack_plan(position, ins, outs):
        at = position[0]
        for j in range(3):
            yield (
                ins[0].at[:, pl.ds(pl.multiple_of(j * D + at * width, width), width)],
                outs[0].at[:part, j * width : (j + 1) * width],
            )
        yield ins[1], outs[0].at[part:, :]
        if aligned:
            for j in range(F):
                yield (
                    ins[2].at[:, pl.ds(pl.multiple_of(j * ff_part + at * ff_own, ff_own), ff_own)],
                    outs[1].at[:part, j * ff_own : (j + 1) * ff_own],
                )
        else:
            yield ins[2], outs[1].at[: up_source.shape[0], :]
        yield (
            ins[3].at[pl.ds(pl.multiple_of(at * ff_own, ff_own), ff_own), :],
            outs[1].at[up_source_rows:, :],
        )

    up_source_rows = part * F * ff_own // D
    qkv_piece, feed_piece = copy_call(
        "pack",
        pack_plan,
        place_now,
        [w_qkv, small_rows, up_source, w_down],
        [(part + extra, wide), (up_source_rows + ff_own, D)],
    )

    docs_row = jnp.pad(segment_ids.astype(BF16), ((0, 15), (0, D - own_rows)))
    packed = jnp.concatenate([hidden, docs_row], axis=0)
    hidden_seen = exchange_seq(jnp.broadcast_to(packed[None], (S, *packed.shape)))
    qkv_pair = spread_fsdp(qkv_piece)
    out_pair = spread_fsdp(after(w_out, *qkv_pair[0]))
    feed_pair = spread_fsdp(after(feed_piece, *out_pair[0]))
    top_parts = gather_seq_parts(after(top, hidden_seen))

    hidden_all = hidden_seen[:, :own_rows].reshape(length, D)
    doc_ids = hidden_seen[:, own_rows, :own_rows].astype(jnp.int32).reshape(1, length)
    doc_col = doc_ids.reshape(length, 1)

    full_qkv, small_all = join_fsdp("join_qkv", qkv_pair, [part, extra])
    full_qkv = full_qkv.reshape(D, wide)
    small_all = small_all.reshape(F, extra * wide)[:, :small_size].astype(F32)
    vectors = [small_all[:, i * part : (i + 1) * part].reshape(D) for i in range(8)]
    gain_one, shift_one, bias_q, bias_v, bias_out, gain_two, shift_two, bias_down = vectors
    bias_up = small_all[:, 8 * part :].reshape(F, S, ff_own)
    bias_up = lax.dynamic_index_in_dim(bias_up, s, 1, keepdims=False).reshape(F * ff_own)

    tokens = hidden.astype(F32)
    xhat_all, unused_rate = stats(hidden_all.astype(F32))
    normed_all = (xhat_all * gain_one + shift_one).astype(BF16)
    own_bias = jnp.concatenate(
        [
            lax.dynamic_slice_in_dim(bias_q, s * width, width),
            jnp.zeros((width,), F32),
            lax.dynamic_slice_in_dim(bias_v, s * width, width),
        ]
    )
    projected = (dot(normed_all, full_qkv) + own_bias).astype(BF16)
    slopes = 2.0 ** (-8.0 * (s * heads + jnp.arange(heads) + 1).astype(F32) / H)
    context, log_total = attention(slopes, projected, doc_col, doc_ids)

    context_seen = exchange_seq(context.reshape(S, own_rows, width))
    gathered = jnp.concatenate([context_seen[k] for k in range(S)], axis=1)
    full_out = join_fsdp("join_out", out_pair, [part])[0].reshape(D, D)
    first_sum = tokens + dot(gathered, full_out) + bias_out
    xhat_two, rate_two = stats(first_sum)
    normed_two = (xhat_two * gain_two + shift_two).astype(BF16)
    normed_two_all = jnp.concatenate(gather_seq_parts(normed_two), axis=0)
    top_all = jnp.concatenate(top_parts, axis=0)
    full_up, full_down = join_fsdp("join_feed", feed_pair, [up_source_rows, ff_own])
    full_up = full_up.reshape(D, F * ff_own)
    full_down = full_down.reshape(F * ff_own, D)
    grad_act = dot(top_all, full_down, NT)
    upward = dot(normed_two_all, full_up) + bias_up
    activated, gelu_back = jax.vjp(lambda u: jax.nn.gelu(u, approximate=True), upward)
    activated = activated.astype(BF16)
    grad_upward = gelu_back(grad_act)[0].astype(BF16)
    grad_normed_two = dot(grad_upward, full_up, NT).astype(BF16)

    def scatter_relative(partial):
        total = partial[:own_rows].astype(F32)
        for k in range(1, S):
            block = partial[k * own_rows : (k + 1) * own_rows].astype(BF16)
            total = total + seq_x(block, k).astype(F32)
        return total

    t_two = scatter_relative(grad_normed_two)
    grad_top = top.astype(F32)
    grad_first = grad_top + norm_back(t_two, xhat_two, rate_two, gain_two)
    grad_attended = grad_first.astype(BF16)
    grad_context = dot(grad_attended, full_out, NT).astype(BF16)
    grad_heads = exchange_seq(
        jnp.stack([grad_context[:, k * width : (k + 1) * width] for k in range(S)])
    ).reshape(length, width)

    def owners(partial, columns):
        return partial.astype(BF16).reshape(F, -1, columns)

    grad_feed = reduce_fsdp(
        [owners(dot(normed_two_all, grad_upward, TN), D), owners(dot(activated, top_all, TN), D)]
    )
    result = first_sum + scatter_relative(dot(activated, full_down)) + bias_down
    output = result.astype(BF16)[None]
    grad_out = reduce_fsdp([owners(dot(gathered, grad_attended, TN), D)])

    grad_projected = attention_back(slopes, projected, grad_heads, doc_col, doc_ids, log_total)
    t_part = dot(grad_projected, full_qkv, NT).astype(BF16)
    t_seen = exchange_seq(t_part.reshape(S, own_rows, D))
    t_one = tree_sum([t_seen[k].astype(F32) for k in range(S)])
    xhat_one, rate_one = stats(tokens)
    grad_input = (grad_first + norm_back(t_one, xhat_one, rate_one, gain_one)).astype(BF16)[None]

    def own_columns(values):
        return put(jnp.zeros((D,), F32), values, s * width).reshape(F, part)

    bias_sums = jnp.sum(grad_projected.astype(F32), axis=0)
    grad_bup = jnp.sum(grad_upward.astype(F32), axis=0).reshape(F, 1, ff_own)
    rows = jnp.concatenate(
        [
            jnp.sum(t_part.astype(F32) * xhat_all, axis=0).reshape(F, part),
            jnp.sum(t_part.astype(F32), axis=0).reshape(F, part),
            own_columns(bias_sums[:width]),
            own_columns(bias_sums[2 * width :]),
            jnp.sum(grad_attended.astype(F32), axis=0).reshape(F, part),
            jnp.sum(t_two * xhat_two, axis=0).reshape(F, part),
            jnp.sum(t_two, axis=0).reshape(F, part),
            jnp.sum(grad_top, axis=0).reshape(F, part),
            put(jnp.zeros((F, S, ff_own), F32), grad_bup, 0, s).reshape(F, ff_part),
        ],
        axis=1,
    )
    rows = jnp.pad(rows, ((0, 0), (0, extra * wide - small_size))).reshape(F, extra, wide)
    grad_qkv = reduce_fsdp(
        [owners(dot(normed_all, grad_projected, TN), wide), rows.astype(BF16)]
    )

    sum_out = tree_sum([p.astype(F32) for p in gather_seq_parts(grad_out.astype(BF16))])
    low = gather_seq_parts(grad_feed.astype(BF16))
    if aligned:
        sum_up, sum_down = pl.pallas_call(
            functools.partial(widen_feed_kernel, up_rows=up_source_rows, blocks=F),
            out_shape=(
                jax.ShapeDtypeStruct((part, F * ff_part), F32),
                jax.ShapeDtypeStruct((ff_part, D), F32),
            ),
            in_specs=[SMEM] + [VMEM] * S,
            out_specs=(VMEM, VMEM),
            compiler_params=pltpu.CompilerParams(vmem_limit_bytes=40 * 2**20),
            name="widen_feed",
        )(place_now, *low)
    else:
        sum_up = jnp.zeros((part, F, S, ff_own), F32)
        sum_down = jnp.zeros((ff_part, D), F32)
        for k in range(S):
            up_k = low[k][:up_source_rows].astype(F32).reshape(part, F, 1, ff_own)
            sum_up = put(sum_up, up_k, 0, 0, s ^ k)
            sum_down = put(sum_down, low[k][up_source_rows:].astype(F32), (s ^ k) * ff_own)
    low = gather_seq_parts(grad_qkv.astype(BF16))
    sum_qkv, mine = pl.pallas_call(
        functools.partial(widen_columns_kernel, blocks=3, rows=part),
        out_shape=(
            jax.ShapeDtypeStruct((part, 3 * D), F32),
            jax.ShapeDtypeStruct((extra, wide), F32),
        ),
        in_specs=[SMEM] + [VMEM] * S,
        out_specs=(VMEM, VMEM),
        compiler_params=pltpu.CompilerParams(vmem_limit_bytes=40 * 2**20),
        name="widen_qkv",
    )(place_now, *low)
    mine = mine.reshape(extra * wide)
    pieces = [mine[i * part : (i + 1) * part] for i in range(8)]

    return (
        output,
        grad_input,
        pieces[0],
        pieces[1],
        sum_qkv,
        jnp.stack([pieces[2], pieces[3]]),
        sum_out,
        pieces[4],
        pieces[5],
        pieces[6],
        sum_up.reshape(part, F * ff_part),
        mine[8 * part : small_size],
        sum_down,
        pieces[7],
    )


def solution(mesh):
    return jax.shard_map(
        functools.partial(body, mesh.shape["seq"], mesh.shape["fsdp"]),
        mesh=mesh,
        in_specs=(
            P("fsdp", "seq", None),
            P("fsdp", "seq"),
            P("fsdp"),
            P("fsdp"),
            P("fsdp", None),
            P(None, "fsdp"),
            P("fsdp", None),
            P("fsdp"),
            P("fsdp"),
            P("fsdp"),
            P("fsdp", None),
            P("fsdp"),
            P("fsdp", None),
            P("fsdp"),
            P("fsdp", "seq", None),
        ),
        out_specs=(
            P("fsdp", "seq", None),
            P("fsdp", "seq", None),
            P("fsdp"),
            P("fsdp"),
            P("fsdp", None),
            P(None, "fsdp"),
            P("fsdp", None),
            P("fsdp"),
            P("fsdp"),
            P("fsdp"),
            P("fsdp", None),
            P("fsdp"),
            P("fsdp", None),
            P("fsdp"),
        ),
        check_vma=False,
    )
```

time: 794 us -> 413 us (0.52)
  waiting for transfers between devices: 382 us -> 202 us
  blocking collectives: 173 us -> 0 us
  matrix products: 123 us -> 34.2 us
  starting transfers between devices: 13 us -> 68 us
  Pallas kernels: 0 us -> 27.8 us
  between operations: 16.4 us -> 1.89 us
    reduce_scatter x4 -> x0, waiting for transfers between devices: 228 us -> none  [owner_rows(): lax.psum_scatter(product_over_rows(left_side, right_side).astype(jnp.bflo...]
    ppermute x0 -> x45, waiting for transfers between devices: none -> 198 us  [the longest x24 113 us: fsdp_x(): return lax.ppermute(x, 'fsdp', [(i, i ^ k) for i in range(F)])]
    all_gather x9 -> x0, blocking collectives: 111 us -> none  [the longest x1 27 us: body(): doc_ids = lax.all_gather(segment_ids, 'seq', axis=1, tiled=True)[0]]
    all_gather x4 -> x0, waiting for transfers between devices: 90.7 us -> none  [the longest x1 60 us: body(): lax.all_gather(w_down, 'fsdp', axis=0, tiled=True)]
    dot_general x26 -> x12, matrix products: 123 us -> 34.2 us  [dot(): return lax.dot_general(a, b, dims, preferred_element_type=F32)]
    psum x1 -> x0, waiting for transfers between devices: 55.7 us -> none  [body(): lax.psum(part_qkv.astype(jnp.bfloat16), 'seq').astype(jnp.float32)]
    ppermute x0 -> x45, starting transfers between devices: none -> 50.2 us  [the longest x21 28.2 us: seq_x(): return lax.ppermute(x, 'seq', [(i, i ^ k) for i in range(S)])]
    all_to_all x1 -> x0, blocking collectives: 27.8 us -> none  [body(): lax.all_to_all(grad_stack, 'seq', split_axis=1, concat_axis=2, tiled=True)]
  transfers between devices with their start and end apart: 13 -> 49, of which waited for: 7 -> 28; matrix products, arithmetic and copies ran while one was open for 20% -> 17% of each run, Pallas kernels for 0% -> 6%
where the time goes in v1:
time: 413 us; the launch traced here: 408 us
  waiting for transfers between devices  202 us (49%)
  starting transfers between devices  68 us (16%)
  local copies, waits for them, and re-layouts  37.9 us (9%)
  other arithmetic  36.7 us (9%)
  matrix products  34.2 us (8%)
  Pallas kernels  27.8 us (7%)
    ppermute x24, waiting for transfers between devices, fsdp_x(): return lax.ppermute(x, 'fsdp', [(i, i ^ k) for i in range(F)])  113 us
    ppermute x21, waiting for transfers between devices, seq_x(): return lax.ppermute(x, 'seq', [(i, i ^ k) for i in range(S)])  84.5 us
    dot_general x12, matrix products, dot(): return lax.dot_general(a, b, dims, preferred_element_type=F32)  34.2 us
    ppermute x21, starting transfers between devices, seq_x(): return lax.ppermute(x, 'seq', [(i, i ^ k) for i in range(S)])  28.2 us
    unnamed x119, local copies, waits for them, and re-layouts  26.3 us
    ppermute x24, starting transfers between devices, fsdp_x(): return lax.ppermute(x, 'fsdp', [(i, i ^ k) for i in range(F)])  22 us
    all_to_all x4, starting transfers between devices, exchange_seq(): return lax.all_to_all(x, 'seq', 0, 0)  17.8 us
    pallas_call x1, Pallas kernels, attention_back(): pl.pallas_call(functools.partial(attention_back_kernel, block=block, long...  10.9 us
  transfers between devices with their start and end apart: 49, of which 28 were waited for; matrix products, arithmetic and copies ran while one was open for 17% of the time, Pallas kernels for 6%

profile of v1, /device:TPU:8, one launch (start us, length us, event | category | flops | bytes accessed | tf_op | source)
XLA Modules:
  0.0 408.4 jit_solution(15233311179160563877)
XLA Ops:
  15.5 5.5 %collective-permute-done.refs_1_ = bf16[144,768]{1,0:T(8,128)(2,1)S(1)} collective-permute-done((bf16[144,768]{1,0:T(8,128)(2,1)S(1)}, bf16[144,768]{1,0:T(8,128)(2,1)S(1)}, u32[]{:S(2)}, u32[]{:S(2)}) %collective-permute-start) | collective-permute-done | bytes 221216 | tf_op jit(solution)/shard_map/ppermute | solution.py:244
  21.0 9.4 %collective-permute-done.1.refs_2_ = bf16[144,768]{1,0:T(8,128)(2,1)S(1)} collective-permute-done((bf16[144,768]{1,0:T(8,128)(2,1)S(1)}, bf16[144,768]{1,0:T(8,128)(2,1)S(1)}, u32[]{:S(2)}, u32[]{:S(2)}) %collective-permute-start.1) | collective-permute-done | bytes 221216 | tf_op jit(solution)/shard_map/ppermute | solution.py:244
  37.4 4.9 %all-to-all-start = ((bf16[4,272,1024]{2,1,0:T(8,128)(2,1)}), bf16[4,272,1024]{2,1,0:T(8,128)(2,1)}, u32[]{:S(2)}, u32[]{:S(2)}) async-start(bf16[4,272,1024]{2,1,0:T(8,128)(2,1)} %broadcast_in_dim.10), calls=%async_computation | async-start | bytes 4456448 | tf_op jit(solution)/shard_map/all_to_all | solution.py:273
  47.1 7.1 %collective-permute-done.4.refs_1_ = bf16[128,1024]{1,0:T(8,128)(2,1)S(1)} collective-permute-done((bf16[128,1024]{1,0:T(8,128)(2,1)S(1)}, bf16[128,1024]{1,0:T(8,128)(2,1)S(1)}, u32[]{:S(2)}, u32[]{:S(2)}) %collective-permute-start.4) | collective-permute-done | bytes 262176 | tf_op jit(solution)/shard_map/ppermute | solution.py:244
  54.2 9.2 %collective-permute-done.5.refs_2_ = bf16[128,1024]{1,0:T(8,128)(2,1)S(1)} collective-permute-done((bf16[128,1024]{1,0:T(8,128)(2,1)S(1)}, bf16[128,1024]{1,0:T(8,128)(2,1)S(1)}, u32[]{:S(2)}, u32[]{:S(2)}) %collective-permute-start.5) | collective-permute-done | bytes 262176 | tf_op jit(solution)/shard_map/ppermute | solution.py:244
  63.4 5.8 %collective-permute-done.6.refs_3_ = bf16[128,1024]{1,0:T(8,128)(2,1)S(1)} collective-permute-done((bf16[128,1024]{1,0:T(8,128)(2,1)S(1)}, bf16[128,1024]{1,0:T(8,128)(2,1)S(1)}, u32[]{:S(2)}, u32[]{:S(2)}) %collective-permute-start.6) | collective-permute-done | bytes 262176 | tf_op jit(solution)/shard_map/ppermute | solution.py:244
  96.1 7.6 %attention.1 = (bf16[1024,256]{1,0:T(8,128)(2,1)S(1)}, f32[4,1024]{1,0:T(4,128)S(1)}) custom-call(f32[4]{0:T(128)S(1)} %multiply_power_fusion.slopes, bf16[1024,768]{1,0:T(8,128)(2,1)S(1)} %add_convert_fusion.2.proj, s32[1024,1]{1,0:T(8,128)S(1)} %copy-done.24, s32[1,1024]{1,0:T(1,128)S(1)} %bitcast.243), custom_call_target="tpu_custom_call" | custom-call | flops 805306368 | bytes 3145728 | tf_op jit(solution)/shard_map/attention/pallas_call | solution.py:109
  109.2 8.3 %collective-permute-done.13.refs_3_ = bf16[256,1024]{1,0:T(8,128)(2,1)S(1)} collective-permute-done((bf16[256,1024]{1,0:T(8,128)(2,1)S(1)}, bf16[256,1024]{1,0:T(8,128)(2,1)S(1)}, u32[]{:S(2)}, u32[]{:S(2)}) %collective-permute-start.13) | collective-permute-done | bytes 524320 | tf_op jit(solution)/shard_map/ppermute | solution.py:244
  131.8 5.3 %collective-permute-done.18 = bf16[256,1024]{1,0:T(8,128)(2,1)} collective-permute-done((bf16[256,1024]{1,0:T(8,128)(2,1)}, bf16[256,1024]{1,0:T(8,128)(2,1)}, u32[]{:S(2)}, u32[]{:S(2)}) %collective-permute-start.18) | collective-permute-done | bytes 524320 | tf_op jit(solution)/shard_map/ppermute | solution.py:241
  138.6 21.6 %collective-permute-done.19 = bf16[256,1024]{1,0:T(8,128)(2,1)} collective-permute-done((bf16[256,1024]{1,0:T(8,128)(2,1)}, bf16[256,1024]{1,0:T(8,128)(2,1)}, u32[]{:S(2)}, u32[]{:S(2)}) %collective-permute-start.19) | collective-permute-done | bytes 524320 | tf_op jit(solution)/shard_map/ppermute | solution.py:241
  178.7 5.3 %convert_reduce_fusion = (bf16[1024]{0:T(1024)(128)(2,1)S(1)}, bf16[1024,1024]{1,0:T(8,128)(2,1)S(1)}) fusion(f32[1024,1024]{1,0:T(8,128)S(1)} %fusion.48, f32[1024]{0:T(1024)S(1)} %fusion.56, bf16[1024,1024]{1,0:T(8,128)(2,1)S(1)} %constant_dynamic-update-slice_fusion, bf16[1024,1024]{1,0:T(8,128)(2,1)S(1)} %bitcast.247), kind=kOutput, calls=%fused_computation.11 | convolution fusion | flops 2171599872 | bytes 10491904 | tf_op jit(solution)/shard_map/dot_general | solution.py:22
  206.6 5.7 %collective-permute-done.16 = bf16[256,1024]{1,0:T(8,128)(2,1)S(1)} collective-permute-done((bf16[256,1024]{1,0:T(8,128)(2,1)S(1)}, bf16[256,1024]{1,0:T(8,128)(2,1)S(1)}, u32[]{:S(2)}, u32[]{:S(2)}) %collective-permute-start.16) | collective-permute-done | bytes 524320 | tf_op jit(solution)/shard_map/ppermute | solution.py:241
  214.4 10.0 %collective-permute-done.21 = bf16[256,1024]{1,0:T(8,128)(2,1)S(1)} collective-permute-done((bf16[256,1024]{1,0:T(8,128)(2,1)S(1)}, bf16[256,1024]{1,0:T(8,128)(2,1)S(1)}, u32[]{:S(2)}, u32[]{:S(2)}) %collective-permute-start.21) | collective-permute-done | bytes 524320 | tf_op jit(solution)/shard_map/ppermute | solution.py:241
  224.5 8.0 %collective-permute-done.22 = bf16[256,1024]{1,0:T(8,128)(2,1)S(1)} collective-permute-done((bf16[256,1024]{1,0:T(8,128)(2,1)S(1)}, bf16[256,1024]{1,0:T(8,128)(2,1)S(1)}, u32[]{:S(2)}, u32[]{:S(2)}) %collective-permute-start.22) | collective-permute-done | bytes 524320 | tf_op jit(solution)/shard_map/ppermute | solution.py:241
  251.1 10.9 %attention_back.1 = bf16[1024,768]{1,0:T(8,128)(2,1)S(1)} custom-call(f32[4]{0:T(128)S(1)} %multiply_power_fusion.slopes, bf16[1024,768]{1,0:T(8,128)(2,1)S(1)} %copy-done.30, bf16[1024,256]{1,0:T(8,128)(2,1)S(1)} %bitcast.240, s32[1024,1]{1,0:T(8,128)S(1)} %copy-done.25, s32[1,1024]{1,0:T(1,128)S(1)} %bitcast.244, f32[4,1024]{1,0:T(4,128)S(1)} %get-tuple-element.39.log_total), custom_call_target="tpu_custom_call" | custom-call | flops 2147483648 | bytes 4718592 | tf_op jit(solution)/shard_map/attention_back/pallas_call | solution.py:131
  262.3 4.9 %multiply_reduce_fusion = (bf16[1024]{0:T(1024)(128)(2,1)S(1)}, bf16[1024,1024]{1,0:T(8,128)(2,1)}, bf16[1024,1024]{1,0:T(8,128)(2,1)}) fusion(f32[1024]{0:T(1024)S(1)} %bitcast.262, f32[1024]{0:T(1024)S(1)} %bitcast.263, bf16[4,272,1024]{2,1,0:T(8,128)(2,1)} %all-to-all-done, f32[1024]{0:T(1024)S(1)} %get-tuple-element.104, ...), kind=kOutput, calls=%fused_computation.12 | convolution fusion | flops 1621097472 | bytes 9455616 | tf_op jit(solution)/shard_map/dot_general | solution.py:22
  286.7 5.8 %collective-permute-done.32 = bf16[128,1024]{1,0:T(8,128)(2,1)S(1)} collective-permute-done((bf16[128,1024]{1,0:T(8,128)(2,1)S(1)}, bf16[128,1024]{1,0:T(8,128)(2,1)S(1)}, u32[]{:S(2)}, u32[]{:S(2)}) %collective-permute-start.32) | collective-permute-done | bytes 262176 | tf_op jit(solution)/shard_map/ppermute | solution.py:244
  295.5 6.7 %collective-permute-done.33 = bf16[128,1024]{1,0:T(8,128)(2,1)S(1)} collective-permute-done((bf16[128,1024]{1,0:T(8,128)(2,1)S(1)}, bf16[128,1024]{1,0:T(8,128)(2,1)S(1)}, u32[]{:S(2)}, u32[]{:S(2)}) %collective-permute-start.33) | collective-permute-done | bytes 262176 | tf_op jit(solution)/shard_map/ppermute | solution.py:244
  302.4 15.7 %collective-permute-done.34 = bf16[128,1024]{1,0:T(8,128)(2,1)S(1)} collective-permute-done((bf16[128,1024]{1,0:T(8,128)(2,1)S(1)}, bf16[128,1024]{1,0:T(8,128)(2,1)S(1)}, u32[]{:S(2)}, u32[]{:S(2)}) %collective-permute-start.34) | collective-permute-done | bytes 262176 | tf_op jit(solution)/shard_map/ppermute | solution.py:244
  346.3 6.6 %collective-permute-done.39 = bf16[256,1024]{1,0:T(8,128)(2,1)} collective-permute-done((bf16[256,1024]{1,0:T(8,128)(2,1)}, bf16[256,1024]{1,0:T(8,128)(2,1)}, u32[]{:S(2)}, u32[]{:S(2)}) %collective-permute-start.39) | collective-permute-done | bytes 524320 | tf_op jit(solution)/shard_map/ppermute | solution.py:244
  352.9 19.1 %collective-permute-done.40 = bf16[256,1024]{1,0:T(8,128)(2,1)} collective-permute-done((bf16[256,1024]{1,0:T(8,128)(2,1)}, bf16[256,1024]{1,0:T(8,128)(2,1)}, u32[]{:S(2)}, u32[]{:S(2)}) %collective-permute-start.40) | collective-permute-done | bytes 524320 | tf_op jit(solution)/shard_map/ppermute | solution.py:244
  372.0 8.6 %collective-permute-done.41 = bf16[256,1024]{1,0:T(8,128)(2,1)} collective-permute-done((bf16[256,1024]{1,0:T(8,128)(2,1)S(1)}, bf16[256,1024]{1,0:T(8,128)(2,1)}, u32[]{:S(2)}, u32[]{:S(2)}) %collective-permute-start.41) | collective-permute-done | bytes 524320 | tf_op jit(solution)/shard_map/ppermute | solution.py:244
  387.4 10.2 %collective-permute-done.42.refs_1_ = bf16[256,1024]{1,0:T(8,128)(2,1)S(1)} collective-permute-done((bf16[256,1024]{1,0:T(8,128)(2,1)S(1)}, bf16[256,1024]{1,0:T(8,128)(2,1)S(1)}, u32[]{:S(2)}, u32[]{:S(2)}) %collective-permute-start.42) | collective-permute-done | bytes 524320 | tf_op jit(solution)/shard_map/ppermute | solution.py:241
  397.6 7.6 %collective-permute-done.43.refs_2_ = bf16[256,1024]{1,0:T(8,128)(2,1)S(1)} collective-permute-done((bf16[256,1024]{1,0:T(8,128)(2,1)S(1)}, bf16[256,1024]{1,0:T(8,128)(2,1)S(1)}, u32[]{:S(2)}, u32[]{:S(2)}) %collective-permute-start.43) | collective-permute-done | bytes 524320 | tf_op jit(solution)/shard_map/ppermute | solution.py:241
  (292 shorter events, 196.4 us)
Async XLA Ops:
  35.6 40.3 %collective-permute-start.3 = (bf16[4,144,768]{2,1,0:T(8,128)(2,1)}, bf16[4,144,768]{2,1,0:T(8,128)(2,1)}, u32[]{:S(2)}, u32[]{:S(2)}) collective-permute-start(bf16[4,144,768]{2,1,0:T(8,128)(2,1)} %pad_maximum_fusion.4), channel_id=1, source_target_pairs={{0,1},{1,0},{2,3},{3,2},{4,5},{5,4},{6,7},{7,6},{8,9},{9,8},{10,11... | collective-permute-start | bytes 2654216 | tf_op jit(solution)/shard_map/ppermute | solution.py:244
  37.4 45.0 %all-to-all-start = ((bf16[4,272,1024]{2,1,0:T(8,128)(2,1)}), bf16[4,272,1024]{2,1,0:T(8,128)(2,1)}, u32[]{:S(2)}, u32[]{:S(2)}) async-start(bf16[4,272,1024]{2,1,0:T(8,128)(2,1)} %broadcast_in_dim.10), calls=%async_computation | async-start | bytes 4456448 | tf_op jit(solution)/shard_map/all_to_all | solution.py:273
  69.2 40.0 %collective-permute-start.11 = (bf16[256,1024]{1,0:T(8,128)(2,1)S(1)}, bf16[256,1024]{1,0:T(8,128)(2,1)S(1)}, u32[]{:S(2)}, u32[]{:S(2)}) collective-permute-start(bf16[256,1024]{1,0:T(8,128)(2,1)S(1)} %get-tuple-element.35.refs_0_), channel_id=1, source_target_pairs={{0,2},{1,3},{2,0},{3,1},{4,6},{5,7},{6,4},{7,5},{8,10},{9,11},{10,... | collective-permute-start | bytes 1572872 | tf_op jit(solution)/shard_map/ppermute | solution.py:244
  69.2 40.0 %collective-permute-start.12 = (bf16[256,1024]{1,0:T(8,128)(2,1)S(1)}, bf16[256,1024]{1,0:T(8,128)(2,1)S(1)}, u32[]{:S(2)}, u32[]{:S(2)}) collective-permute-start(bf16[256,1024]{1,0:T(8,128)(2,1)S(1)} %get-tuple-element.35.refs_0_), channel_id=1, source_target_pairs={{0,4},{1,5},{2,6},{3,7},{4,0},{5,1},{6,2},{7,3},{8,12},{9,13},{10,... | collective-permute-start | bytes 1572872 | tf_op jit(solution)/shard_map/ppermute | solution.py:244
  72.3 45.2 %collective-permute-start.13 = (bf16[256,1024]{1,0:T(8,128)(2,1)S(1)}, bf16[256,1024]{1,0:T(8,128)(2,1)S(1)}, u32[]{:S(2)}, u32[]{:S(2)}) collective-permute-start(bf16[256,1024]{1,0:T(8,128)(2,1)S(1)} %get-tuple-element.35.refs_0_), channel_id=1, source_target_pairs={{0,6},{1,7},{2,4},{3,5},{4,2},{5,3},{6,0},{7,1},{8,14},{9,15},{10,... | collective-permute-start | bytes 1572872 | tf_op jit(solution)/shard_map/ppermute | solution.py:244
  76.0 43.2 %collective-permute-start.7 = (bf16[4,128,1024]{2,1,0:T(8,128)(2,1)}, bf16[4,128,1024]{2,1,0:T(8,128)(2,1)S(1)}, u32[]{:S(2)}, u32[]{:S(2)}) collective-permute-start(bf16[4,128,1024]{2,1,0:T(8,128)(2,1)} %pad_maximum_fusion.3), channel_id=1, source_target_pairs={{0,1},{1,0},{2,3},{3,2},{4,5},{5,4},{6,7},{7,6},{8,9},{9,8},{10,11... | collective-permute-start | bytes 3145736 | tf_op jit(solution)/shard_map/ppermute | solution.py:244
  119.1 47.2 %collective-permute-start.14 = (bf16[4,256,1024]{2,1,0:T(8,128)(2,1)}, bf16[4,256,1024]{2,1,0:T(8,128)(2,1)}, u32[]{:S(2)}, u32[]{:S(2)}) collective-permute-start(bf16[4,256,1024]{2,1,0:T(8,128)(2,1)} %pad_maximum_fusion.1), channel_id=1, source_target_pairs={{0,1},{1,0},{2,3},{3,2},{4,5},{5,4},{6,7},{7,6},{8,9},{9,8},{10,11... | collective-permute-start | bytes 6291464 | tf_op jit(solution)/shard_map/ppermute | solution.py:244
  123.5 36.7 %collective-permute-start.19 = (bf16[256,1024]{1,0:T(8,128)(2,1)}, bf16[256,1024]{1,0:T(8,128)(2,1)}, u32[]{:S(2)}, u32[]{:S(2)}) collective-permute-start(bf16[256,1024]{1,0:T(8,128)(2,1)} %bitcast.40), channel_id=1, source_target_pairs={{0,16},{8,24},{16,0},{24,8},{1,17},{9,25},{17,1},{25,9},{2,18},{10... | collective-permute-start | bytes 1572872 | tf_op jit(solution)/shard_map/ppermute | solution.py:241
  125.0 40.2 %collective-permute-start.20 = (bf16[256,1024]{1,0:T(8,128)(2,1)}, bf16[256,1024]{1,0:T(8,128)(2,1)}, u32[]{:S(2)}, u32[]{:S(2)}) collective-permute-start(bf16[256,1024]{1,0:T(8,128)(2,1)} %bitcast.40), channel_id=1, source_target_pairs={{0,24},{8,16},{16,8},{24,0},{1,25},{9,17},{17,9},{25,1},{2,26},{10... | collective-permute-start | bytes 1572872 | tf_op jit(solution)/shard_map/ppermute | solution.py:241
  129.4 38.8 %collective-permute-start.10 = (bf16[256,1024]{1,0:T(8,128)(2,1)S(1)}, bf16[256,1024]{1,0:T(8,128)(2,1)S(1)}, u32[]{:S(2)}, u32[]{:S(2)}) collective-permute-start(bf16[256,1024]{1,0:T(8,128)(2,1)S(1)} %add_convert_fusion.6), channel_id=1, source_target_pairs={{0,24},{8,16},{16,8},{24,0},{1,25},{9,17},{17,9},{25,1},{2,26},{10... | collective-permute-start | bytes 1572872 | tf_op jit(solution)/shard_map/ppermute | solution.py:241
  137.1 33.2 %collective-permute-start.8 = (bf16[256,1024]{1,0:T(8,128)(2,1)S(1)}, bf16[256,1024]{1,0:T(8,128)(2,1)S(1)}, u32[]{:S(2)}, u32[]{:S(2)}) collective-permute-start(bf16[256,1024]{1,0:T(8,128)(2,1)S(1)} %add_convert_fusion.6), channel_id=1, source_target_pairs={{0,8},{8,0},{16,24},{24,16},{1,9},{9,1},{17,25},{25,17},{2,10},{10... | collective-permute-start | bytes 1572872 | tf_op jit(solution)/shard_map/ppermute | solution.py:241
  187.1 25.2 %collective-permute-start.16 = (bf16[256,1024]{1,0:T(8,128)(2,1)S(1)}, bf16[256,1024]{1,0:T(8,128)(2,1)S(1)}, u32[]{:S(2)}, u32[]{:S(2)}) collective-permute-start(bf16[256,1024]{1,0:T(8,128)(2,1)S(1)} %get-tuple-element.73), channel_id=1, source_target_pairs={{0,16},{8,24},{16,0},{24,8},{1,17},{9,25},{17,1},{25,9},{2,18},{10... | collective-permute-start | bytes 1572872 | tf_op jit(solution)/shard_map/ppermute | solution.py:241
  188.9 25.5 %collective-permute-start.17 = (bf16[256,1024]{1,0:T(8,128)(2,1)S(1)}, bf16[256,1024]{1,0:T(8,128)(2,1)S(1)}, u32[]{:S(2)}, u32[]{:S(2)}) collective-permute-start(bf16[256,1024]{1,0:T(8,128)(2,1)S(1)} %get-tuple-element.72), channel_id=1, source_target_pairs={{0,24},{8,16},{16,8},{24,0},{1,25},{9,17},{17,9},{25,1},{2,26},{10... | collective-permute-start | bytes 1572872 | tf_op jit(solution)/shard_map/ppermute | solution.py:241
  193.1 31.4 %collective-permute-start.21 = (bf16[256,1024]{1,0:T(8,128)(2,1)S(1)}, bf16[256,1024]{1,0:T(8,128)(2,1)S(1)}, u32[]{:S(2)}, u32[]{:S(2)}) collective-permute-start(bf16[256,1024]{1,0:T(8,128)(2,1)S(1)} %get-tuple-element.68), channel_id=1, source_target_pairs={{0,8},{8,0},{16,24},{24,16},{1,9},{9,1},{17,25},{25,17},{2,10},{10... | collective-permute-start | bytes 1572872 | tf_op jit(solution)/shard_map/ppermute | solution.py:241
  193.4 39.0 %collective-permute-start.22 = (bf16[256,1024]{1,0:T(8,128)(2,1)S(1)}, bf16[256,1024]{1,0:T(8,128)(2,1)S(1)}, u32[]{:S(2)}, u32[]{:S(2)}) collective-permute-start(bf16[256,1024]{1,0:T(8,128)(2,1)S(1)} %get-tuple-element.70), channel_id=1, source_target_pairs={{0,16},{8,24},{16,0},{24,8},{1,17},{9,25},{17,1},{25,9},{2,18},{10... | collective-permute-start | bytes 1572872 | tf_op jit(solution)/shard_map/ppermute | solution.py:241
  201.9 32.4 %collective-permute-start.23 = (bf16[256,1024]{1,0:T(8,128)(2,1)S(1)}, bf16[256,1024]{1,0:T(8,128)(2,1)S(1)}, u32[]{:S(2)}, u32[]{:S(2)}) collective-permute-start(bf16[256,1024]{1,0:T(8,128)(2,1)S(1)} %get-tuple-element.69), channel_id=1, source_target_pairs={{0,24},{8,16},{16,8},{24,0},{1,25},{9,17},{17,9},{25,1},{2,26},{10... | collective-permute-start | bytes 1572872 | tf_op jit(solution)/shard_map/ppermute | solution.py:241
  212.3 116.6 %collective-permute-start.38 = (bf16[4,256,1024]{2,1,0:T(8,128)(2,1)}, bf16[4,256,1024]{2,1,0:T(8,128)(2,1)}, u32[]{:S(2)}, u32[]{:S(2)}) collective-permute-start(bf16[4,256,1024]{2,1,0:T(8,128)(2,1)} %pad_maximum_fusion.2), channel_id=1, source_target_pairs={{0,1},{1,0},{2,3},{3,2},{4,5},{5,4},{6,7},{7,6},{8,9},{9,8},{10,11... | collective-permute-start | bytes 6291464 | tf_op jit(solution)/shard_map/ppermute | solution.py:244
  245.7 33.6 %collective-permute-start.31 = (bf16[4,128,1024]{2,1,0:T(8,128)(2,1)}, bf16[4,128,1024]{2,1,0:T(8,128)(2,1)}, u32[]{:S(2)}, u32[]{:S(2)}) collective-permute-start(bf16[4,128,1024]{2,1,0:T(8,128)(2,1)} %dynamic-slice_bitcast_fusion.4), channel_id=1, source_target_pairs={{0,1},{1,0},{2,3},{3,2},{4,5},{5,4},{6,7},{7,6},{8,9},{9,8},{10,11... | collective-permute-start | bytes 3145736 | tf_op jit(solution)/shard_map/ppermute | solution.py:244
  274.8 69.3 %all-to-all-start.3 = ((bf16[4,256,1024]{2,1,0:T(8,128)(2,1)}), bf16[4,256,1024]{2,1,0:T(8,128)(2,1)}, u32[]{:S(2)}, u32[]{:S(2)}) async-start(bf16[4,256,1024]{2,1,0:T(8,128)(2,1)} %bitcast.46), calls=%async_computation.3 | async-start | bytes 4194304 | tf_op jit(solution)/shard_map/all_to_all | solution.py:273
  284.1 34.0 %collective-permute-start.34 = (bf16[128,1024]{1,0:T(8,128)(2,1)S(1)}, bf16[128,1024]{1,0:T(8,128)(2,1)S(1)}, u32[]{:S(2)}, u32[]{:S(2)}) collective-permute-start(bf16[128,1024]{1,0:T(8,128)(2,1)S(1)} %get-tuple-element.60), channel_id=1, source_target_pairs={{0,6},{1,7},{2,4},{3,5},{4,2},{5,3},{6,0},{7,1},{8,14},{9,15},{10,... | collective-permute-start | bytes 786440 | tf_op jit(solution)/shard_map/ppermute | solution.py:244
  285.7 35.8 %collective-permute-start.25 = (bf16[144,768]{1,0:T(8,128)(2,1)S(1)}, bf16[144,768]{1,0:T(8,128)(2,1)S(1)}, u32[]{:S(2)}, u32[]{:S(2)}) collective-permute-start(bf16[144,768]{1,0:T(8,128)(2,1)S(1)} %get-tuple-element.74), channel_id=1, source_target_pairs={{0,2},{1,3},{2,0},{3,1},{4,6},{5,7},{6,4},{7,5},{8,10},{9,11},{10,... | collective-permute-start | bytes 663560 | tf_op jit(solution)/shard_map/ppermute | solution.py:244
  292.5 30.4 %collective-permute-start.26 = (bf16[144,768]{1,0:T(8,128)(2,1)S(1)}, bf16[144,768]{1,0:T(8,128)(2,1)S(1)}, u32[]{:S(2)}, u32[]{:S(2)}) collective-permute-start(bf16[144,768]{1,0:T(8,128)(2,1)S(1)} %get-tuple-element.75), channel_id=1, source_target_pairs={{0,4},{1,5},{2,6},{3,7},{4,0},{5,1},{6,2},{7,3},{8,12},{9,13},{10,... | collective-permute-start | bytes 663560 | tf_op jit(solution)/shard_map/ppermute | solution.py:244
  334.9 37.1 %collective-permute-start.40 = (bf16[256,1024]{1,0:T(8,128)(2,1)}, bf16[256,1024]{1,0:T(8,128)(2,1)}, u32[]{:S(2)}, u32[]{:S(2)}) collective-permute-start(bf16[256,1024]{1,0:T(8,128)(2,1)} %get-tuple-element.57), channel_id=1, source_target_pairs={{0,4},{1,5},{2,6},{3,7},{4,0},{5,1},{6,2},{7,3},{8,12},{9,13},{10,... | collective-permute-start | bytes 1572872 | tf_op jit(solution)/shard_map/ppermute | solution.py:244
  337.8 42.8 %collective-permute-start.41 = (bf16[256,1024]{1,0:T(8,128)(2,1)S(1)}, bf16[256,1024]{1,0:T(8,128)(2,1)}, u32[]{:S(2)}, u32[]{:S(2)}) collective-permute-start(bf16[256,1024]{1,0:T(8,128)(2,1)S(1)} %get-tuple-element.58), channel_id=1, source_target_pairs={{0,6},{1,7},{2,4},{3,5},{4,2},{5,3},{6,0},{7,1},{8,14},{9,15},{10,... | collective-permute-start | bytes 1572872 | tf_op jit(solution)/shard_map/ppermute | solution.py:244
  (74 other events, 716.0 us)
